TPU v7x, 32 devices: a whole 2x2x4 slice. The times are simulated.
32 devices in a mesh: row: 8 (over z, x), col: 4 (over y, core).
Axes of the slice: x: 2, y: 2, z: 4, core: 2. Of those that a mesh axis runs over, the one named last changes fastest.
Arguments:
- inputs: bfloat16 [1024, 6144], P('col', 'row'), may hold values from -6 to 6
- out_grad: bfloat16 [1024, 6144], P('col', 'row'), may hold values from -6 to 6
- pre_act: bfloat16 [1024, 24576], P('row', 'col'), may hold values from -8 to 8
- w_in: bfloat16 [6144, 24576], P('row', 'col'), may hold values from -0.078125 to 0.078125
- w_out: bfloat16 [24576, 6144], P('col', 'row'), may hold values from -0.0390625 to 0.0390625
Outputs:
- in_grad: bfloat16 [1024, 6144], P('col', 'row')
- w_in_grad: bfloat16 [6144, 24576], P('row', 'col')
- w_out_grad: bfloat16 [24576, 6144], P('col', 'row')
All inputs are finite; a program needn't handle non-finite values.
Results may differ from a plain program's by a relative error of at most 0.03.
Values may be sent and summed in bfloat16 or wider, within the bound.
A program may use at most 128 MiB of HBM per device.

v0:
```python
import jax
import jax.numpy as jnp
from jax import lax
from jax.sharding import PartitionSpec as P


def gelu_parts(pre_act):
    value = pre_act.astype(jnp.float32)
    cumul = 0.5 * (1.0 + jax.scipy.special.erf(value * 0.7071067811865476))
    density = jnp.exp(-0.5 * value * value) * 0.3989422804014327
    return (value * cumul, cumul + value * density)


def on_device(inputs, out_grad, pre_act, w_in, w_out):
    inputs_all, grad_all = (
        lax.all_gather(inputs, "col", axis=0, tiled=True),
        lax.all_gather(out_grad, "col", axis=0, tiled=True),
    )
    block = grad_all
    total = lax.psum(
        lax.dot_general(
            block, w_out, (((1,), (1,)), ((), ())), preferred_element_type=jnp.float32
        ).astype(jnp.bfloat16),
        "row",
    ).astype(jnp.float32)
    pre_all = lax.all_gather(pre_act, "row", axis=0, tiled=True)
    value, slope = gelu_parts(pre_all)
    hidden = value.astype(jnp.bfloat16)
    pre_grad = (total * slope).astype(jnp.bfloat16)
    w_out_grad = lax.dot_general(
        hidden, grad_all, (((0,), (0,)), ((), ())), preferred_element_type=jnp.float32
    ).astype(jnp.bfloat16)
    w_in_grad = lax.dot_general(
        inputs_all, pre_grad, (((0,), (0,)), ((), ())), preferred_element_type=jnp.float32
    ).astype(jnp.bfloat16)
    block = pre_grad
    in_grad = lax.psum_scatter(
        lax.dot_general(
            block, w_in, (((1,), (1,)), ((), ())), preferred_element_type=jnp.float32
        ).astype(jnp.bfloat16),
        "col",
        scatter_dimension=0,
        tiled=True,
    )
    return (in_grad, w_in_grad, w_out_grad)


def solution(mesh):
    in_specs = (P("col", "row"), P("col", "row"), P("row", "col"), P("row", "col"), P("col", "row"))
    out_specs = (P("col", "row"), P("row", "col"), P("col", "row"))
    return jax.shard_map(
        on_device, mesh=mesh, in_specs=in_specs, out_specs=out_specs, check_vma=False
    )
```

profile of v0, /device:TPU:0, one launch (start us, length us, event | category | flops | bytes accessed | tf_op | source)
XLA Modules:
  0.0 706.6 jit_solution(9485560660195165470)
XLA Ops:
  7.2 0.0 all-gather.4.cloned.1.call-start
  7.2 0.7 all-gather.4.cloned.1.call-update
  7.9 0.0 all-reduce.2.cloned.1.call-start
  7.9 24.0 %all-gather.4.cloned.1.call-done = bf16[1024,768]{1,0:T(8,128)(2,1)} async-done(((bf16[256,768]{1,0:T(8,128)(2,1)}), bf16[1024,768]{1,0:T(8,128)(2,1)}) %all-gather.4.cloned.1.call-update) | async-done | bytes 1572880 | tf_op jit(solution)/shard_map/all_gather | solution.py:17
  32.0 15.7 %convolution_convert_fusion = bf16[1024,6144]{1,0:T(8,128)(2,1)} fusion(bf16[1024,768]{1,0:T(8,128)(2,1)} %all-gather.4.cloned.1.call-done, bf16[6144,768]{1,0:T(8,128)(2,1)} %param.9), kind=kOutput, calls=%fused_computation.15 | convolution fusion | flops 9669967872 | bytes 23592960 | tf_op jit(solution)/shard_map/dot_general | solution.py:21
  47.6 0.0 all-reduce.2.cloned.1.call-update
  47.6 0.0 all-gather.6.cloned.1.call-start
  47.7 0.7 all-gather.6.cloned.1.call-update
  48.4 0.0 all-gather.8.cloned.1.call-start
  48.4 0.5 all-gather.8.cloned.1.call-update
  49.0 0.2 reduce-scatter.2.cloned.1.call-start
  49.2 396.2 %all-reduce.2.cloned.1.call-done = bf16[1024,6144]{1,0:T(8,128)(2,1)} async-done(((bf16[1024,6144]{1,0:T(8,128)(2,1)}), bf16[1024,6144]{1,0:T(8,128)(2,1)}) %all-reduce.2.cloned.1.call-update) | async-done | bytes 12582928 | tf_op jit(solution)/shard_map/psum | solution.py:20
  445.4 178.0 %all-gather.6.cloned.1.call-done = bf16[1024,6144]{1,0:T(8,128)(2,1)} async-done(((bf16[128,6144]{1,0:T(8,128)(2,1)}), bf16[1024,6144]{1,0:T(8,128)(2,1)}) %all-gather.6.cloned.1.call-update) | async-done | bytes 12582928 | tf_op jit(solution)/shard_map/all_gather | solution.py:26
  623.4 13.7 %fusion.7 = bf16[1024,6144]{1,0:T(8,128)(2,1)S(1)} fusion(bf16[1024,6144]{1,0:T(8,128)(2,1)} %all-gather.6.cloned.1.call-done, bf16[1024,6144]{1,0:T(8,128)(2,1)} %all-reduce.2.cloned.1.call-done), kind=kLoop, calls=%fused_computation.12 | loop fusion | flops 75497472 | bytes 37748736 | tf_op jit(solution)/shard_map/convert_element_type | solution.py:29
  637.1 0.0 copy-start
  637.1 4.5 copy-done
  641.6 13.2 %convolution_convert_fusion.2 = bf16[1024,768]{1,0:T(8,128)(2,1)} fusion(bf16[1024,6144]{1,0:T(8,128)(2,1)S(1)} %fusion.7, bf16[768,6144]{1,0:T(8,128)(2,1)} %param.8), kind=kOutput, calls=%fused_computation.19 | convolution fusion | flops 9664462848 | bytes 23592960 | tf_op jit(solution)/shard_map/dot_general | solution.py:38
  654.7 0.0 reduce-scatter.2.cloned.1.call-update
  654.8 0.0 all-gather.8.cloned.1.call-done
  654.8 15.8 %fusion.14 = bf16[768,6144]{0,1:T(8,128)(2,1)} fusion(bf16[1024,6144]{1,0:T(8,128)(2,1)} %copy-done, bf16[1024,768]{1,0:T(8,128)(2,1)} %all-gather.8.cloned.1.call-done), kind=kOutput, calls=%fused_computation.18 | convolution fusion | flops 9668395008 | bytes 23592960 | tf_op jit(solution)/shard_map/dot_general | solution.py:33
  670.6 0.0 copy-start.1
  670.6 12.8 %copy.8 = bf16[768,6144]{1,0:T(8,128)(2,1)} copy(bf16[768,6144]{0,1:T(8,128)(2,1)} %fusion.14) | data formatting | bytes 18874368
  683.3 0.0 copy-done.1
  683.3 16.7 %fusion.11 = bf16[6144,768]{1,0:T(8,128)(2,1)} fusion(bf16[1024,768]{1,0:T(8,128)(2,1)S(1)} %copy-done.1, bf16[1024,6144]{1,0:T(8,128)(2,1)} %all-gather.6.cloned.1.call-done), kind=kOutput, calls=%fused_computation.16 | convolution fusion | flops 9706143744 | bytes 23592960 | tf_op jit(solution)/shard_map/dot_general | solution.py:30
  (1 shorter events, 0.0 us)
Async XLA Ops:
  7.2 24.8 %all-gather.4.cloned.1.call-start = ((), (), s32[]{:S(2)}) async-start(), calls=%async_computation.1 | async-start | bytes 1966080 | tf_op jit(solution)/shard_map/all_gather | solution.py:17
  7.9 437.5 %all-reduce.2.cloned.1.call-start = ((), (), s32[]{:S(2)}) async-start(), calls=%async_computation.2 | async-start | bytes 25165824 | tf_op jit(solution)/shard_map/psum | solution.py:20
  47.6 575.8 %all-gather.6.cloned.1.call-start = ((), (), s32[]{:S(2)}) async-start(), calls=%async_computation.3 | async-start | bytes 14155776 | tf_op jit(solution)/shard_map/all_gather | solution.py:26
  48.4 606.4 %all-gather.8.cloned.1.call-start = ((), (), s32[]{:S(2)}) async-start(), calls=%async_computation.5 | async-start | bytes 1966080 | tf_op jit(solution)/shard_map/all_gather | solution.py:16
  49.0 651.1 %reduce-scatter.2.cloned.1.call-start = ((), (), s32[]{:S(2)}) async-start(), calls=%async_computation.4 | async-start | bytes 1966080 | tf_op jit(solution)/shard_map/reduce_scatter | solution.py:37
  637.1 4.5 copy-start
  670.6 12.8 %copy-start.1 = (bf16[1024,768]{1,0:T(8,128)(2,1)S(1)}, bf16[1024,768]{1,0:T(8,128)(2,1)}, u32[]{:S(2)}) copy-start(bf16[1024,768]{1,0:T(8,128)(2,1)} %all-gather.4.cloned.1.call-done) | copy-start | bytes 4718596
Sparse Core Ops, SparseCore 0:
  9.6 22.3 all-gather.3
  47.8 397.6 all-reduce.1
  447.9 175.5 all-gather.5
  624.9 17.8 all-gather.7
  654.9 26.3 reduce-scatter.1
where the time goes:
time: 707 us
  waiting for transfers between devices  600 us (85%)
  matrix products  61.3 us (9%)
  local copies, waits for them, and re-layouts  17.2 us (2%)
  between operations  13.8 us (2%)
  other arithmetic  13.7 us (2%)
    psum x1, waiting for transfers between devices, on_device(): lax.psum(lax.dot_general(block, w_out, (((1,), (1,)), ((), ())), preferre...  396 us
    all_gather x1, waiting for transfers between devices, on_device(): pre_all = lax.all_gather(pre_act, 'row', axis=0, tiled=True)  178 us
    all_gather x1, waiting for transfers between devices, on_device(): lax.all_gather(out_grad, 'col', axis=0, tiled=True)  24 us
    unnamed x5, local copies, waits for them, and re-layouts  17.2 us
    dot_general x1, matrix products, on_device(): lax.dot_general(hidden, grad_all, (((0,), (0,)), ((), ())), preferred_ele...  16.7 us
    dot_general x1, matrix products, on_device(): lax.dot_general(inputs_all, pre_grad, (((0,), (0,)), ((), ())), preferred...  15.8 us
    dot_general x1, matrix products, on_device(): lax.dot_general(block, w_out, (((1,), (1,)), ((), ())), preferred_element...  15.7 us
  transfers between devices with their start and end apart: 5, of which 3 were waited for; matrix products, arithmetic and copies ran while one was open for 10% of the time, Pallas kernels for 0%

commit v1 on v0

v1 whole, which is shorter than its diff:
```python
import functools

import jax
import jax.numpy as jnp
from jax import lax
from jax.experimental import pallas as pl
from jax.experimental.pallas import tpu as pltpu
from jax.sharding import PartitionSpec as P

MESH = pl.DeviceIdType.MESH
CHIPS_Z = 4
PIECES = 2
TILE = 512


def gelu_parts(pre_act):
    value = pre_act.astype(jnp.float32)
    cumul = 0.5 * (1.0 + jax.scipy.special.erf(value * 0.7071067811865476))
    density = jnp.exp(-0.5 * value * value) * 0.3989422804014327
    return (value * cumul, cumul + value * density)


def row_at(place, n_row):
    across = n_row // CHIPS_Z
    x, z = place // CHIPS_Z, place % CHIPS_Z
    z = z + (x % 2) * (CHIPS_Z - 1 - 2 * z)
    return z * across + x


def place_of(row, n_row):
    across = n_row // CHIPS_Z
    x, z = row % across, row // across
    return x * CHIPS_Z + z + (x % 2) * (CHIPS_Z - 1 - 2 * z)


def ring_kernel(
    n_row, n_col,
    hid_ref, slope_ref, og_ref, in_ref, wout_ref,
    hid_all, pg_all, g_all, i_all,
    wv, gv, part, rbuf, pgv, sv,
    local_sem, csend, crecv, hsend, hrecv, rsend, rrecv, psend, precv,
):
    row, col = lax.axis_index("row"), lax.axis_index("col")
    place = place_of(row, n_row)
    ahead = row_at((place + 1) % n_row, n_row)
    behind = row_at((place + n_row - 1) % n_row, n_row)
    targets = (ahead, behind)
    tb, ff = hid_ref.shape
    tc = og_ref.shape[0]
    rw = tb // (2 * PIECES)
    steps = n_row - 1
    lanes = [(d, c) for c in range(PIECES) for d in range(2)]

    def block_at(d, s):
        at = (place + n_row - s) % n_row if d == 0 else (place + s) % n_row
        return row_at(at, n_row)

    def rows_of(block, d, c):
        return pl.ds(pl.multiple_of(block * tb + (d * PIECES + c) * rw, 16), rw)

    def own(d, c):
        return pl.ds((d * PIECES + c) * rw, rw)

    barrier = pltpu.get_barrier_semaphore()
    for target in targets:
        pl.semaphore_signal(barrier, 1, device_id=(target, col), device_id_type=MESH)
    for off in range(1, n_col):
        pl.semaphore_signal(
            barrier, 1, device_id=(row, (col + off) % n_col), device_id_type=MESH
        )
    pl.semaphore_wait(barrier, n_col + 1)

    def gather_copy(source, full, send, recv, d, c, s):
        block = block_at(d, s)
        src = source.at[own(d, c)] if source is not None else full.at[rows_of(block, d, c)]
        return pltpu.make_async_remote_copy(
            src_ref=src, dst_ref=full.at[rows_of(block, d, c)],
            send_sem=send.at[d, c, s], recv_sem=recv.at[d, c, s],
            device_id=(targets[d], col), device_id_type=MESH,
        )

    def sum_copy(d, c, s):
        block = block_at(d, s + 1)
        return pltpu.make_async_remote_copy(
            src_ref=part.at[rows_of(block, d, c)], dst_ref=rbuf.at[s, own(d, c)],
            send_sem=rsend.at[d, c, s], recv_sem=rrecv.at[d, c, s],
            device_id=(targets[d], col), device_id_type=MESH,
        )

    def col_copy(which, off):
        mine = pl.ds(pl.multiple_of(col * tc, 16), tc)
        return pltpu.make_async_remote_copy(
            src_ref=(og_ref, in_ref)[which], dst_ref=(gv, i_all)[which].at[mine],
            send_sem=csend.at[which, off - 1], recv_sem=crecv.at[which, off - 1],
            device_id=(row, (col + off) % n_col), device_id_type=MESH,
        )

    for d, c in lanes:
        gather_copy(hid_ref, hid_all, hsend, hrecv, d, c, 0).start()
    for which in range(2):
        for off in range(1, n_col):
            col_copy(which, off).start()
    mine = pl.ds(pl.multiple_of(col * tc, 16), tc)
    mine_row = pl.ds(pl.multiple_of(row * tb, 16), tb)
    local = [
        pltpu.make_async_copy(og_ref, gv.at[mine], local_sem.at[0]),
        pltpu.make_async_copy(wout_ref, wv, local_sem.at[1]),
        pltpu.make_async_copy(slope_ref, sv, local_sem.at[2]),
        pltpu.make_async_copy(in_ref, i_all.at[mine], local_sem.at[3]),
        pltpu.make_async_copy(hid_ref, hid_all.at[mine_row], local_sem.at[4]),
    ]
    for copy in local:
        copy.start()

    def hid_step(s):
        for d, c in lanes:
            gather_copy(None, hid_all, hsend, hrecv, d, c, s - 1).wait_recv()
            gather_copy(None, hid_all, hsend, hrecv, d, c, s).start()

    n_tiles = ff // TILE
    early = min(2, steps - 1)
    per_step = -(-n_tiles // (steps - 1 - early))

    @pl.loop(1, 1 + early)
    def _(s):
        hid_step(s)

    for copy in local:
        copy.wait()
    for which in range(2):
        for off in range(1, n_col):
            col_copy(which, off).wait_recv()

    g_out = pltpu.make_async_copy(gv, g_all, local_sem.at[5])
    g_out.start()

    def partial_tile(t):
        at = pl.ds(pl.multiple_of(t * TILE, TILE), TILE)
        part[:, at] = lax.dot_general(
            gv[...], wv[at, :], (((1,), (1,)), ((), ())), preferred_element_type=jnp.float32
        ).astype(jnp.bfloat16)

    @pl.loop(1 + early, steps)
    def _(s):
        hid_step(s)
        first = (s - 1 - early) * per_step

        @pl.loop(0, per_step)
        def _(k):
            @pl.when(first + k < n_tiles)
            def _():
                partial_tile(first + k)

    for d, c in lanes:
        sum_copy(d, c, 0).start()
    for d, c in lanes:
        gather_copy(None, hid_all, hsend, hrecv, d, c, steps - 1).wait_recv()

    @pl.loop(1, steps)
    def _(s):
        for d, c in lanes:
            sum_copy(d, c, s - 1).wait_recv()
            at = rows_of(block_at(d, s + 1), d, c)
            total = part[at, :].astype(jnp.float32) + rbuf[s - 1, own(d, c), :].astype(jnp.float32)
            part[at, :] = total.astype(jnp.bfloat16)
            sum_copy(d, c, s).start()

    for d, c in lanes:
        sum_copy(d, c, steps - 1).wait_recv()
        at = rows_of(row, d, c)
        total = part[at, :].astype(jnp.float32) + rbuf[steps - 1, own(d, c), :].astype(jnp.float32)
        pgv[own(d, c), :] = (total * sv[own(d, c), :]).astype(jnp.bfloat16)
        gather_copy(pgv, pg_all, psend, precv, d, c, 0).start()
    p_out = pltpu.make_async_copy(pgv, pg_all.at[mine_row], local_sem.at[6])
    p_out.start()

    @pl.loop(1, steps)
    def _(s):
        for d, c in lanes:
            gather_copy(None, pg_all, psend, precv, d, c, s - 1).wait_recv()
            gather_copy(None, pg_all, psend, precv, d, c, s).start()

    for d, c in lanes:
        gather_copy(None, pg_all, psend, precv, d, c, steps - 1).wait_recv()
    p_out.wait()
    g_out.wait()

    @pl.loop(0, steps)
    def _(s):
        for d, c in lanes:
            gather_copy(None, hid_all, hsend, hrecv, d, c, s).wait_send()
            sum_copy(d, c, s).wait_send()
            gather_copy(None, pg_all, psend, precv, d, c, s).wait_send()

    for which in range(2):
        for off in range(1, n_col):
            col_copy(which, off).wait_send()


def on_device(n_row, n_col, inputs, out_grad, pre_act, w_in, w_out):
    value, slope = gelu_parts(pre_act)
    hidden = value.astype(jnp.bfloat16)
    tb, ff = pre_act.shape
    tc, width = inputs.shape
    tokens, steps = tb * n_row, n_row - 1
    anywhere = pl.BlockSpec(memory_space=pl.ANY)
    lanes = pltpu.SemaphoreType.DMA((2, PIECES, steps))
    bf16 = jnp.bfloat16
    hidden_all, pre_grad, grad_all, inputs_all = pl.pallas_call(
        functools.partial(ring_kernel, n_row, n_col),
        out_shape=[
            jax.ShapeDtypeStruct((tokens, ff), bf16),
            jax.ShapeDtypeStruct((tokens, ff), bf16),
            jax.ShapeDtypeStruct((tokens, width), bf16),
            jax.ShapeDtypeStruct((tokens, width), bf16),
        ],
        in_specs=[anywhere] * 5,
        out_specs=[anywhere] * 4,
        scratch_shapes=[
            pltpu.VMEM((ff, width), bf16),
            pltpu.VMEM((tokens, width), bf16),
            pltpu.VMEM((tokens, ff), bf16),
            pltpu.VMEM((steps, tb, ff), bf16),
            pltpu.VMEM((tb, ff), bf16),
            pltpu.VMEM((tb, ff), jnp.float32),
            pltpu.SemaphoreType.DMA((7,)),
            pltpu.SemaphoreType.DMA((2, n_col - 1)),
            pltpu.SemaphoreType.DMA((2, n_col - 1)),
            lanes, lanes, lanes, lanes, lanes, lanes,
        ],
        compiler_params=pltpu.CompilerParams(
            collective_id=0, has_side_effects=True, vmem_limit_bytes=56 * 2**20
        ),
        name="ring",
    )(hidden, slope, out_grad, inputs, w_out)
    in_grad = lax.psum_scatter(
        lax.dot_general(
            pre_grad, w_in, (((1,), (1,)), ((), ())), preferred_element_type=jnp.float32
        ).astype(bf16),
        "col",
        scatter_dimension=0,
        tiled=True,
    )
    w_out_grad = lax.dot_general(
        hidden_all, grad_all, (((0,), (0,)), ((), ())), preferred_element_type=jnp.float32
    ).astype(bf16)
    w_in_grad = lax.dot_general(
        inputs_all, pre_grad, (((0,), (0,)), ((), ())), preferred_element_type=jnp.float32
    ).astype(bf16)
    return (in_grad, w_in_grad, w_out_grad)


def solution(mesh):
    in_specs = (P("col", "row"), P("col", "row"), P("row", "col"), P("row", "col"), P("col", "row"))
    out_specs = (P("col", "row"), P("row", "col"), P("col", "row"))
    return jax.shard_map(
        functools.partial(on_device, mesh.shape["row"], mesh.shape["col"]),
        mesh=mesh, in_specs=in_specs, out_specs=out_specs, check_vma=False,
    )
```

time: 707 us -> 440 us (0.62)
  waiting for transfers between devices: 600 us -> 0.02 us
  Pallas kernels: 0 us -> 372 us
  local copies, waits for them, and re-layouts: 17.2 us -> 0.01 us
  matrix products: 61.3 us -> 49.9 us
  other arithmetic: 13.7 us -> 4.01 us
    psum x1 -> x0, waiting for transfers between devices: 396 us -> none  [on_device(): lax.psum(lax.dot_general(block, w_out, (((1,), (1,)), ((), ())), preferre...]
    pallas_call x0 -> x1, Pallas kernels: none -> 372 us  [on_device(): pl.pallas_call(functools.partial(ring_kernel, n_row, n_col), out_shape=[j...]
    all_gather x3 -> x0, waiting for transfers between devices: 202 us -> none  [the longest x1 178 us: on_device(): pre_all = lax.all_gather(pre_act, 'row', axis=0, tiled=True)]
    unnamed x5 -> x4, local copies, waits for them, and re-layouts: 17.2 us -> 0.01 us
    convert_element_type x1 -> x0, other arithmetic: 13.7 us -> none  [on_device(): pre_grad = (total * slope).astype(jnp.bfloat16)]
    dot_general x3 -> x2, matrix products: 45.6 us -> 33 us  [the longest x1 17.2 us: on_device(): lax.dot_general(hidden_all, grad_all, (((0,), (0,)), ((), ())), preferred...]
  transfers between devices with their start and end apart: 5 -> 1, of which waited for: 3 -> 0; matrix products, arithmetic and copies ran while one was open for 10% -> 8% of each run, Pallas kernels for 0% -> 0%
where the time goes in v1:
time: 440 us
  Pallas kernels  372 us (85%)
  matrix products  49.9 us (11%)
  between operations  14.1 us (3%)
    pallas_call x1, Pallas kernels, on_device(): pl.pallas_call(functools.partial(ring_kernel, n_row, n_col), out_shape=[j...  372 us
    dot_general x1, matrix products, on_device(): lax.dot_general(hidden_all, grad_all, (((0,), (0,)), ((), ())), preferred...  17.2 us
    dot_general x1, matrix products, on_device(): lax.dot_general(inputs_all, pre_grad, (((0,), (0,)), ((), ())), preferred...  16.9 us
    dot_general x1, matrix products, on_device(): lax.dot_general(pre_grad, w_in, (((1,), (1,)), ((), ())), preferred_eleme...  15.8 us
  transfers between devices with their start and end apart: 1, of which 0 were waited for; matrix products, arithmetic and copies ran while one was open for 8% of the time, Pallas kernels for 0%

profile of v1, /device:TPU:0, one launch (start us, length us, event | category | flops | bytes accessed | tf_op | source)
XLA Modules:
  0.0 439.7 jit_solution(5686731839800651778)
XLA Ops:
  7.2 0.0 reduce-scatter.2.cloned.1.call-start
  7.2 4.0 fusion.6
  11.2 371.7 %ring.1 = (bf16[1024,6144]{1,0:T(8,128)(2,1)}, bf16[1024,6144]{1,0:T(8,128)(2,1)}, bf16[1024,768]{1,0:T(8,128)(2,1)}, bf16[1024,768]{1,0:T(8,128)(2,1)}) custom-call(bf16[128,6144]{1,0:T(8,128)(2,1)} %get-tuple-element.12.hid_ref, f32[128,6144]{1,0:T(8,128)} %get-tuple-element.11.slope_ref, bf16[256,768]{1,0:T(8,128)(2,1)} %og_ref.1, ...), custom_call_target="tpu_custom_call" | custom-call | tf_op jit(solution)/shard_map/ring/pallas_call | solution.py:209
  382.9 0.0 copy-start.1
  383.0 15.8 %convolution_convert_fusion.2 = bf16[1024,768]{1,0:T(8,128)(2,1)} fusion(bf16[1024,6144]{1,0:T(8,128)(2,1)} %get-tuple-element.7, bf16[768,6144]{1,0:T(8,128)(2,1)} %param.8), kind=kOutput, calls=%fused_computation.14 | convolution fusion | flops 9664462848 | bytes 23592960 | tf_op jit(solution)/shard_map/dot_general | solution.py:237
  398.8 0.0 reduce-scatter.2.cloned.1.call-update
  398.8 0.0 copy-done.1
  398.8 0.0 copy-start
  398.8 16.9 %convolution_convert_fusion = bf16[768,6144]{1,0:T(8,128)(2,1)} fusion(bf16[1024,768]{1,0:T(8,128)(2,1)S(1)} %copy-done.1, bf16[1024,6144]{1,0:T(8,128)(2,1)} %get-tuple-element.7), kind=kOutput, calls=%fused_computation | convolution fusion | flops 9668395008 | bytes 23592960 | tf_op jit(solution)/shard_map/dot_general | solution.py:247
  415.7 0.0 copy-done
  415.7 17.2 %convolution_convert_fusion.1 = bf16[6144,768]{1,0:T(8,128)(2,1)} fusion(bf16[1024,6144]{1,0:T(8,128)(2,1)} %get-tuple-element.9, bf16[1024,768]{1,0:T(8,128)(2,1)S(1)} %copy-done), kind=kOutput, calls=%fused_computation.1 | convolution fusion | flops 9668395008 | bytes 23592960 | tf_op jit(solution)/shard_map/dot_general | solution.py:244
  432.9 0.0 reduce-scatter.2.cloned.1.call-done
Async XLA Ops:
  7.2 425.7 %reduce-scatter.2.cloned.1.call-start = ((), (), s32[]{:S(2)}) async-start(), calls=%async_computation.1 | async-start | bytes 1966080 | tf_op jit(solution)/shard_map/reduce_scatter | solution.py:236
  382.9 15.8 %copy-start.1 = (bf16[1024,768]{1,0:T(8,128)(2,1)S(1)}, bf16[1024,768]{1,0:T(8,128)(2,1)}, u32[]{:S(2)}) copy-start(bf16[1024,768]{1,0:T(8,128)(2,1)} %get-tuple-element.8) | copy-start | bytes 4718596
  398.8 16.9 %copy-start = (bf16[1024,768]{1,0:T(8,128)(2,1)S(1)}, bf16[1024,768]{1,0:T(8,128)(2,1)}, u32[]{:S(2)}) copy-start(bf16[1024,768]{1,0:T(8,128)(2,1)} %get-tuple-element.10) | copy-start | bytes 4718596
Sparse Core Ops, SparseCore 0:
  398.9 27.7 reduce-scatter.1
